TPU v7x, 32 devices: a whole 2x2x4 slice. The times are simulated.
32 devices in a mesh: wide: 16 (over z, y, core), narrow: 2 (over x).
Axes of the slice: x: 2, y: 2, z: 4, core: 2. Of those that a mesh axis runs over, the one named last changes fastest.
Arguments:
- right_side: float32 [96, 128, 256], P(('wide', 'narrow')), may hold values from -6 to 6
- diag_inverse: float32 [96, 128, 128], P(('wide', 'narrow')), may hold values from -1 to 1, as said below
- off_tiles: float32 [96, 48, 128, 128], P('wide', 'narrow'), may hold values from -0.078125 to 0.078125
- tile_columns: int32 [96, 48], P('wide', 'narrow'), may hold values from 0 to 95, as said below
- colors: int32 [96], replicated, may hold values from 0 to 2, as said below
Outputs:
- potentials: float32 [96, 128, 256], P(('wide', 'narrow'))
Inputs may be any that keep to these rules, and one draw needn't show every extreme that they name: `colors`: each device along wide+narrow owns 3 consecutive blocks, exactly 1 of each color. `tile_columns`: slot k of a block row names a block owned by a device whose narrow index is k // 24, and of another color than the row's block. `diag_inverse`: symmetric tiles.
All inputs are finite; a program needn't handle non-finite values.
Results may differ from a plain program's by a relative error of at most 0.0001.
Values sent between devices are 32-bit elements; how exact they have to be, the bound alone decides.
A program may use at most 128 MiB of HBM per device.

v0:
```python
from functools import partial
import jax
import jax.numpy as jnp
from jax import lax
from jax.sharding import PartitionSpec as P


def block_terms(stack, tile_rows, column_slots, column_hues, start, count):
    picked = stack[column_hues, column_slots]
    return jnp.einsum("rkab,rkbl->ral", tile_rows, picked, precision=lax.Precision.HIGHEST)


def sweep(source, sorted_inv, sorted_tiles, slot_of, color_of, wide_size, narrow_size, per_color):
    label_width = source.shape[2]
    tile_size = source.shape[1]
    copies = jnp.zeros((3, wide_size * per_color, tile_size, label_width), jnp.float32)
    pieces = [None, None, None]
    for section, color_now in enumerate((0, 1, 2, 1, 0)):
        offset = color_now * per_color
        local_side = source[offset : offset + per_color]
        if section > 0:
            row_low = color_now * narrow_size * per_color
            row_high = row_low + narrow_size * per_color
            term_fn = partial(
                block_terms,
                copies,
                sorted_tiles[row_low:row_high],
                slot_of[row_low:row_high],
                color_of[row_low:row_high],
            )
            summed = lax.psum_scatter(
                term_fn(jnp.int32(0), lax.axis_size("narrow") * per_color),
                "narrow",
                scatter_dimension=0,
                tiled=True,
            )
            local_side = local_side - summed
        updated = jnp.einsum(
            "rab,rbl->ral",
            sorted_inv[offset : offset + per_color],
            local_side,
            precision=lax.Precision.HIGHEST,
        )
        pieces[color_now] = updated
        if section < 4:
            gathered = lax.all_gather(updated, "wide", axis=0, tiled=True)
            copies = copies.at[color_now].set(gathered)
    return jnp.concatenate(pieces, axis=0)


def shards(right_side, diag_inverse, off_tiles, tile_columns, colors):
    wide_size = lax.axis_size("wide")
    narrow_size = lax.axis_size("narrow")
    wide_at = lax.axis_index("wide")
    narrow_at = lax.axis_index("narrow")
    row_count = off_tiles.shape[0]
    own_count = right_side.shape[0]
    per_color = own_count // 3
    block_total = colors.shape[0]
    row_colors = lax.dynamic_slice_in_dim(colors, wide_at * row_count, row_count)
    row_order = jnp.argsort(row_colors, stable=True)
    sorted_tiles = off_tiles[row_order]
    sorted_cols = tile_columns[row_order]
    owner_colors = colors.reshape(block_total // own_count, own_count)
    owner_order = jnp.argsort(owner_colors, axis=1, stable=True)
    owner_inverse = jnp.argsort(owner_order, axis=1)
    ranks = (owner_inverse - owner_colors * per_color).reshape(block_total)
    block_ids = jnp.arange(block_total, dtype=jnp.int32)
    slot_all = block_ids // (narrow_size * own_count) * per_color + ranks
    slot_of = slot_all[sorted_cols]
    color_of = colors[sorted_cols]
    own_start = (wide_at * narrow_size + narrow_at) * own_count
    own_colors = lax.dynamic_slice_in_dim(colors, own_start, own_count)
    own_order = jnp.argsort(own_colors, stable=True)
    own_inverse = jnp.argsort(own_order)
    sorted_inv = diag_inverse[own_order]
    sorted_side = right_side[own_order]
    result = sweep(
        sorted_side, sorted_inv, sorted_tiles, slot_of, color_of, wide_size, narrow_size, per_color
    )
    return result[own_inverse]


def solution(mesh):
    return jax.shard_map(
        shards,
        mesh=mesh,
        in_specs=(
            P(("wide", "narrow"), None, None),
            P(("wide", "narrow"), None, None),
            P("wide", "narrow", None, None),
            P("wide", "narrow"),
            P(),
        ),
        out_specs=P(("wide", "narrow"), None, None),
        check_vma=False,
    )
```

profile of v0, /device:TPU:0, one launch (start us, length us, event | category | flops | bytes accessed | tf_op | source)
XLA Modules:
  0.0 317.8 jit_solution(14142655278700782819)
XLA Ops:
  6.5 0.8 dynamic_slice.6
  7.3 0.7 sort.85
  8.1 0.6 gather_fusion.1
  8.7 1.5 gather_fusion
  10.2 0.9 fusion.8
  11.2 0.8 reshape.195
  11.9 0.7 dynamic_slice.7
  12.7 1.0 sort.86
  13.7 1.2 gather_fusion.3
  15.1 0.6 sort.87
  15.8 0.6 sort.88
  16.4 0.1 copy.8
  16.5 0.1 reshape.196
  16.6 1.9 gather_fusion.4
  18.6 1.6 gather_fusion.5
  20.2 0.1 reshape.297
  20.3 0.1 reshape.295
  20.4 0.1 reshape.253
  20.5 8.6 %gather_fusion.2 = f32[6,24,128,128]{3,2,1,0:T(8,128)} fusion(f32[6,24,128,128]{3,2,1,0:T(8,128)} %param.15, s32[1024]{0:T(1024)S(1)} %pad_clamp_fusion.2), kind=kCustom, calls=%fused_computation.2 | custom fusion | bytes 18874392 | tf_op jit(solution)/shard_map/gather | solution.py:62
  29.1 26.3 %all-gather.9.cloned.1.call-done = f32[2048,256]{1,0:T(8,128)} async-done(((f32[128,256]{1,0:T(8,128)}), f32[2048,256]{1,0:T(8,128)}) %all-gather.9.cloned.1.call-update) | async-done | bytes 2097168 | tf_op jit(solution)/shard_map/all_gather | solution.py:46
  55.4 5.1 %scatter.14 = f32[3,16,128,256]{3,2,1,0:T(8,128)} pad(f32[1,16,128,256]{3,2,1,0:T(8,128)} %bitcast.69, f32[]{:T(128)} %constant.133.clone.1), padding=0_2x0_0x0_0x0_0 | pad | bytes 8388612 | tf_op jit(solution)/shard_map/scatter | solution.py:47
  60.4 6.5 %gather_fusion.6 = f32[48,128,256]{2,1,0:T(8,128)} fusion(f32[3,16,128,256]{3,2,1,0:T(8,128)} %scatter.14, s32[48]{0:T(128)S(1)} %reshape.253), kind=kCustom, calls=%fused_computation.6 | custom fusion | bytes 12583296 | tf_op jit(solution)/shard_map/gather | solution.py:9
  66.9 9.7 %convolution_bitcast_fusion.3 = f32[2,128,256]{2,1,0:T(8,128)} fusion(f32[6,24,128,128]{3,2,1,0:T(8,128)} %gather_fusion.2, f32[2,24,128,256]{3,2,1,0:T(8,128)} %bitcast.65), kind=kOutput, calls=%fused_computation.14 | convolution fusion | flops 2415919104 | bytes 15990784 | tf_op jit(solution)/shard_map/rkab,rkbl->ral/dot_general | solution.py:10
  76.7 10.5 %reduce-scatter.5.cloned.1.call-done = f32[1,128,256]{2,1,0:T(8,128)} async-done(((f32[2,128,256]{2,1,0:T(8,128)}), f32[1,128,256]{2,1,0:T(8,128)}) %reduce-scatter.5.cloned.1.call-update) | async-done | bytes 131088 | tf_op jit(solution)/shard_map/reduce_scatter | solution.py:31
  87.3 1.8 fusion.6
  89.3 0.1 reshape.259
  89.4 41.7 %all-gather.11.cloned.1.call-done = f32[2048,256]{1,0:T(8,128)} async-done(((f32[128,256]{1,0:T(8,128)}), f32[2048,256]{1,0:T(8,128)}) %all-gather.11.cloned.1.call-update) | async-done | bytes 2097168 | tf_op jit(solution)/shard_map/all_gather | solution.py:46
  131.1 3.2 %constant_dynamic-update-slice_fusion.2 = f32[3,16,128,256]{3,2,1,0:T(8,128)} fusion(f32[3,16,128,256]{3,2,1,0:T(8,128)} %scatter.14, f32[1,16,128,256]{3,2,1,0:T(8,128)} %bitcast.67), kind=kLoop, calls=%fused_computation.72 | loop fusion | bytes 4194304 | tf_op jit(solution)/shard_map/scatter | solution.py:47
  134.3 6.5 %gather_fusion.7 = f32[48,128,256]{2,1,0:T(8,128)} fusion(f32[3,16,128,256]{3,2,1,0:T(8,128)} %constant_dynamic-update-slice_fusion.2, s32[48]{0:T(128)S(1)} %reshape.259), kind=kCustom, calls=%fused_computation.7 | custom fusion | bytes 12583296 | tf_op jit(solution)/shard_map/gather | solution.py:9
  140.8 9.7 %convolution_bitcast_fusion.2 = f32[2,128,256]{2,1,0:T(8,128)} fusion(f32[6,24,128,128]{3,2,1,0:T(8,128)} %gather_fusion.2, f32[2,24,128,256]{3,2,1,0:T(8,128)} %bitcast.63), kind=kOutput, calls=%fused_computation.13 | convolution fusion | flops 2415919104 | bytes 15990784 | tf_op jit(solution)/shard_map/rkab,rkbl->ral/dot_general | solution.py:10
  150.6 10.5 %reduce-scatter.7.cloned.1.call-done = f32[1,128,256]{2,1,0:T(8,128)} async-done(((f32[2,128,256]{2,1,0:T(8,128)}), f32[1,128,256]{2,1,0:T(8,128)}) %reduce-scatter.7.cloned.1.call-update) | async-done | bytes 131088 | tf_op jit(solution)/shard_map/reduce_scatter | solution.py:31
  161.2 1.8 fusion.1
  163.0 0.2 reduce-scatter.9.cloned.1.call-start
  163.2 41.4 %all-gather.13.cloned.1.call-done = f32[2048,256]{1,0:T(8,128)} async-done(((f32[128,256]{1,0:T(8,128)}), f32[2048,256]{1,0:T(8,128)}) %all-gather.13.cloned.1.call-update) | async-done | bytes 2097168 | tf_op jit(solution)/shard_map/all_gather | solution.py:46
  204.6 3.1 constant_dynamic-update-slice_fusion.1
  207.7 6.5 %gather_fusion.8 = f32[48,128,256]{2,1,0:T(8,128)} fusion(f32[3,16,128,256]{3,2,1,0:T(8,128)} %constant_dynamic-update-slice_fusion.1, s32[48]{0:T(128)S(1)} %reshape.253), kind=kCustom, calls=%fused_computation.8 | custom fusion | bytes 12583296 | tf_op jit(solution)/shard_map/gather | solution.py:9
  214.2 9.7 %convolution_bitcast_fusion.1 = f32[2,128,256]{2,1,0:T(8,128)} fusion(f32[6,24,128,128]{3,2,1,0:T(8,128)} %gather_fusion.2, f32[2,24,128,256]{3,2,1,0:T(8,128)} %bitcast.64), kind=kOutput, calls=%fused_computation.12 | convolution fusion | flops 2415919104 | bytes 15990784 | tf_op jit(solution)/shard_map/rkab,rkbl->ral/dot_general | solution.py:10
  224.0 10.5 %reduce-scatter.9.cloned.1.call-done = f32[1,128,256]{2,1,0:T(8,128)} async-done(((f32[2,128,256]{2,1,0:T(8,128)}), f32[1,128,256]{2,1,0:T(8,128)}) %reduce-scatter.9.cloned.1.call-update) | async-done | bytes 131088 | tf_op jit(solution)/shard_map/reduce_scatter | solution.py:31
  234.5 1.8 fusion.4
  236.6 0.1 reshape.271
  236.7 41.7 %all-gather.15.cloned.1.call-done = f32[2048,256]{1,0:T(8,128)} async-done(((f32[128,256]{1,0:T(8,128)}), f32[2048,256]{1,0:T(8,128)}) %all-gather.15.cloned.1.call-update) | async-done | bytes 2097168 | tf_op jit(solution)/shard_map/all_gather | solution.py:46
  278.4 3.2 %constant_dynamic-update-slice_fusion = f32[3,16,128,256]{3,2,1,0:T(8,128)} fusion(f32[3,16,128,256]{3,2,1,0:T(8,128)} %constant_dynamic-update-slice_fusion.1, f32[1,16,128,256]{3,2,1,0:T(8,128)} %bitcast.66), kind=kLoop, calls=%fused_computation.70 | loop fusion | bytes 4194304 | tf_op jit(solution)/shard_map/scatter | solution.py:47
  281.6 6.5 %gather_fusion.9 = f32[48,128,256]{2,1,0:T(8,128)} fusion(f32[3,16,128,256]{3,2,1,0:T(8,128)} %constant_dynamic-update-slice_fusion, s32[48]{0:T(128)S(1)} %reshape.271), kind=kCustom, calls=%fused_computation.9 | custom fusion | bytes 12583296 | tf_op jit(solution)/shard_map/gather | solution.py:9
  288.1 9.8 %convolution_bitcast_fusion = f32[2,128,256]{2,1,0:T(8,128)} fusion(f32[6,24,128,128]{3,2,1,0:T(8,128)} %gather_fusion.2, f32[2,24,128,256]{3,2,1,0:T(8,128)} %bitcast.62), kind=kOutput, calls=%fused_computation.11 | convolution fusion | flops 2415919104 | bytes 15990784 | tf_op jit(solution)/shard_map/rkab,rkbl->ral/dot_general | solution.py:10
  297.9 0.7 sort.89
  298.6 9.8 %reduce-scatter.11.cloned.1.call-done = f32[1,128,256]{2,1,0:T(8,128)} async-done(((f32[2,128,256]{2,1,0:T(8,128)}), f32[1,128,256]{2,1,0:T(8,128)}) %reduce-scatter.11.cloned.1.call-update) | async-done | bytes 131088 | tf_op jit(solution)/shard_map/reduce_scatter | solution.py:31
  308.5 1.2 convolution_bitcast_fusion.4
  309.7 1.3 gather_fusion.10
  (48 shorter events, 1.2 us)
Async XLA Ops:
  6.5 1.6 copy-start
  6.5 48.8 %all-gather.9.cloned.1.call-start = ((), (), s32[]{:S(2)}) async-start(), calls=%async_computation.8 | async-start | bytes 2228224 | tf_op jit(solution)/shard_map/all_gather | solution.py:46
  11.1 76.2 %reduce-scatter.5.cloned.1.call-start = ((), (), s32[]{:S(2)}) async-start(), calls=%async_computation.4 | async-start | bytes 393216 | tf_op jit(solution)/shard_map/reduce_scatter | solution.py:31
  76.7 54.4 %all-gather.11.cloned.1.call-start = ((), (), s32[]{:S(2)}) async-start(), calls=%async_computation.9 | async-start | bytes 2228224 | tf_op jit(solution)/shard_map/all_gather | solution.py:46
  89.1 72.1 %reduce-scatter.7.cloned.1.call-start = ((), (), s32[]{:S(2)}) async-start(), calls=%async_computation.5 | async-start | bytes 393216 | tf_op jit(solution)/shard_map/reduce_scatter | solution.py:31
  150.6 54.0 %all-gather.13.cloned.1.call-start = ((), (), s32[]{:S(2)}) async-start(), calls=%async_computation.10 | async-start | bytes 2228224 | tf_op jit(solution)/shard_map/all_gather | solution.py:46
  163.0 71.5 %reduce-scatter.9.cloned.1.call-start = ((), (), s32[]{:S(2)}) async-start(), calls=%async_computation.6 | async-start | bytes 393216 | tf_op jit(solution)/shard_map/reduce_scatter | solution.py:31
  223.9 54.4 %all-gather.15.cloned.1.call-start = ((), (), s32[]{:S(2)}) async-start(), calls=%async_computation.11 | async-start | bytes 2228224 | tf_op jit(solution)/shard_map/all_gather | solution.py:46
  236.4 72.1 %reduce-scatter.11.cloned.1.call-start = ((), (), s32[]{:S(2)}) async-start(), calls=%async_computation.7 | async-start | bytes 393216 | tf_op jit(solution)/shard_map/reduce_scatter | solution.py:31
  288.1 21.6 %copy-start.1 = (f32[128,256]{1,0:T(8,128)S(1)}, f32[128,256]{1,0:T(8,128)}, u32[]{:S(2)}) copy-start(f32[128,256]{1,0:T(8,128)} %fusion.1) | copy-start | bytes 393220
  288.1 21.6 %copy-start.2 = (f32[128,256]{1,0:T(8,128)S(1)}, f32[128,256]{1,0:T(8,128)}, u32[]{:S(2)}) copy-start(f32[128,256]{1,0:T(8,128)} %fusion.4) | copy-start | bytes 393220
Sparse Core Ops, SparseCore 0:
  11.2 44.0 all-gather.8
  76.8 10.4 reduce-scatter.4
  89.7 41.4 all-gather.10
  150.7 10.4 reduce-scatter.6
  163.2 41.3 all-gather.12
  224.1 10.4 reduce-scatter.8
  236.9 41.4 all-gather.14
  298.0 10.4 reduce-scatter.10
where the time goes:
time: 318 us
  waiting for transfers between devices  193 us (61%)
  local copies, waits for them, and re-layouts  60.7 us (19%)
  matrix products  46.6 us (15%)
  between operations  13.6 us (4%)
  other arithmetic  3.94 us (1%)
    all_gather x4, waiting for transfers between devices, sweep(): gathered = lax.all_gather(updated, 'wide', axis=0, tiled=True)  151 us
    reduce_scatter x4, waiting for transfers between devices, sweep(): lax.psum_scatter(term_fn(jnp.int32(0), lax.axis_size('narrow') * per_colo...  41.4 us
    dot_general x4, matrix products, block_terms(): jnp.einsum('rkab,rkbl->ral', tile_rows, picked, precision=lax.Precision.H...  39 us
    gather x4, local copies, waits for them, and re-layouts, block_terms(): picked = stack[column_hues, column_slots]  26 us
    scatter x4, local copies, waits for them, and re-layouts, sweep(): copies = copies.at[color_now].set(gathered)  14.5 us
    gather x1, local copies, waits for them, and re-layouts, shards(): sorted_tiles = off_tiles[row_order]  8.58 us
    dot_general x5, matrix products, sweep(): jnp.einsum('rab,rbl->ral', sorted_inv[offset:offset + per_color], local_s...  7.55 us
  transfers between devices with their start and end apart: 8, of which 8 were waited for; matrix products, arithmetic and copies ran while one was open for 6% of the time, Pallas kernels for 0%

commit v1 on v0

--- a/solution.py
+++ b/solution.py
@@ -1,8 +1,24 @@
+import functools
 from functools import partial
 import jax
 import jax.numpy as jnp
 from jax import lax
 from jax.sharding import PartitionSpec as P
+
+
+def review_body_up(mat, dimension_no):
+    n = lax.axis_size("wide")
+    buffers = [(tick, (tick + 1) % n) for tick in range(n)]
+    current_arr = [None] * n
+    current_arr[n - 1] = mat
+    for hop_no in range(n - 2, -1, -1):
+        current_arr[hop_no] = lax.ppermute(current_arr[hop_no + 1], axis_name="wide", perm=buffers)
+    block_now = jnp.concatenate(current_arr, dimension_no)
+    carry = (lax.axis_index("wide") + 1) * mat.shape[dimension_no]
+    return jnp.roll(block_now, carry, dimension_no)
+
+
+take_routes_all_all = functools.partial(review_body_up, dimension_no=0)
 
 
 def block_terms(stack, tile_rows, column_slots, column_hues, start, count):
@@ -43,7 +59,7 @@
         )
         pieces[color_now] = updated
         if section < 4:
-            gathered = lax.all_gather(updated, "wide", axis=0, tiled=True)
+            gathered = take_routes_all_all(updated)
             copies = copies.at[color_now].set(gathered)
     return jnp.concatenate(pieces, axis=0)
 

time: 318 us -> 568 us (1.79)
  waiting for transfers between devices: 193 us -> 449 us
  local copies, waits for them, and re-layouts: 60.7 us -> 50 us
  other arithmetic: 3.94 us -> 9.7 us
    ppermute x0 -> x60, waiting for transfers between devices: none -> 412 us  [review_body_up(): lax.ppermute(current_arr[hop_no + 1], axis_name='wide', perm=buffers)]
    all_gather x4 -> x0, waiting for transfers between devices: 151 us -> none  [sweep(): gathered = lax.all_gather(updated, 'wide', axis=0, tiled=True)]
    scatter x4 -> x1, local copies, waits for them, and re-layouts: 14.5 us -> 3.36 us  [sweep(): copies = copies.at[color_now].set(gathered)]
  transfers between devices with their start and end apart: 8 -> 64, of which waited for: 8 -> 63; matrix products, arithmetic and copies ran while one was open for 6% -> 3% of each run, Pallas kernels for 0% -> 0%
where the time goes in v1:
time: 568 us; the launch traced here: 567 us
  waiting for transfers between devices  449 us (79%)
  local copies, waits for them, and re-layouts  50 us (9%)
  matrix products  43.9 us (8%)
  between operations  13.9 us (2%)
  other arithmetic  9.7 us (2%)
    ppermute x60, waiting for transfers between devices, review_body_up(): lax.ppermute(current_arr[hop_no + 1], axis_name='wide', perm=buffers)  412 us
    dot_general x4, matrix products, block_terms(): jnp.einsum('rkab,rkbl->ral', tile_rows, picked, precision=lax.Precision.H...  39 us
    reduce_scatter x4, waiting for transfers between devices, sweep(): lax.psum_scatter(term_fn(jnp.int32(0), lax.axis_size('narrow') * per_colo...  36.2 us
    gather x4, local copies, waits for them, and re-layouts, block_terms(): picked = stack[column_hues, column_slots]  26.1 us
  transfers between devices with their start and end apart: 64, of which 63 were waited for; matrix products, arithmetic and copies ran while one was open for 3% of the time, Pallas kernels for 0%

profile of v1, /device:TPU:0, one launch (start us, length us, event | category | flops | bytes accessed | tf_op | source)
XLA Modules:
  0.0 567.0 jit_solution(9997540870178803604)
XLA Ops:
  14.0 7.6 %collective-permute-done = f32[1,128,256]{2,1,0:T(8,128)S(1)} collective-permute-done((f32[1,128,256]{2,1,0:T(8,128)S(1)}, f32[1,128,256]{2,1,0:T(8,128)S(1)}, u32[]{:S(2)}, u32[]{:S(2)}) %collective-permute-start) | collective-permute-done | bytes 131104 | tf_op jit(solution)/shard_map/ppermute | solution.py:15
  21.6 7.1 %collective-permute-done.1 = f32[1,128,256]{2,1,0:T(8,128)S(1)} collective-permute-done((f32[1,128,256]{2,1,0:T(8,128)S(1)}, f32[1,128,256]{2,1,0:T(8,128)S(1)}, u32[]{:S(2)}, u32[]{:S(2)}) %collective-permute-start.1) | collective-permute-done | bytes 131104 | tf_op jit(solution)/shard_map/ppermute | solution.py:15
  28.7 7.1 %collective-permute-done.2 = f32[1,128,256]{2,1,0:T(8,128)S(1)} collective-permute-done((f32[1,128,256]{2,1,0:T(8,128)S(1)}, f32[1,128,256]{2,1,0:T(8,128)S(1)}, u32[]{:S(2)}, u32[]{:S(2)}) %collective-permute-start.2) | collective-permute-done | bytes 131104 | tf_op jit(solution)/shard_map/ppermute | solution.py:15
  35.8 7.1 %collective-permute-done.3 = f32[1,128,256]{2,1,0:T(8,128)S(1)} collective-permute-done((f32[1,128,256]{2,1,0:T(8,128)S(1)}, f32[1,128,256]{2,1,0:T(8,128)S(1)}, u32[]{:S(2)}, u32[]{:S(2)}) %collective-permute-start.3) | collective-permute-done | bytes 131104 | tf_op jit(solution)/shard_map/ppermute | solution.py:15
  42.9 7.1 %collective-permute-done.4 = f32[1,128,256]{2,1,0:T(8,128)S(1)} collective-permute-done((f32[1,128,256]{2,1,0:T(8,128)S(1)}, f32[1,128,256]{2,1,0:T(8,128)S(1)}, u32[]{:S(2)}, u32[]{:S(2)}) %collective-permute-start.4) | collective-permute-done | bytes 131104 | tf_op jit(solution)/shard_map/ppermute | solution.py:15
  50.0 7.1 %collective-permute-done.5 = f32[1,128,256]{2,1,0:T(8,128)S(1)} collective-permute-done((f32[1,128,256]{2,1,0:T(8,128)S(1)}, f32[1,128,256]{2,1,0:T(8,128)S(1)}, u32[]{:S(2)}, u32[]{:S(2)}) %collective-permute-start.5) | collective-permute-done | bytes 131104 | tf_op jit(solution)/shard_map/ppermute | solution.py:15
  57.1 7.1 %collective-permute-done.6 = f32[1,128,256]{2,1,0:T(8,128)S(1)} collective-permute-done((f32[1,128,256]{2,1,0:T(8,128)S(1)}, f32[1,128,256]{2,1,0:T(8,128)S(1)}, u32[]{:S(2)}, u32[]{:S(2)}) %collective-permute-start.6) | collective-permute-done | bytes 131104 | tf_op jit(solution)/shard_map/ppermute | solution.py:15
  64.2 7.1 %collective-permute-done.7 = f32[1,128,256]{2,1,0:T(8,128)S(1)} collective-permute-done((f32[1,128,256]{2,1,0:T(8,128)S(1)}, f32[1,128,256]{2,1,0:T(8,128)S(1)}, u32[]{:S(2)}, u32[]{:S(2)}) %collective-permute-start.7) | collective-permute-done | bytes 131104 | tf_op jit(solution)/shard_map/ppermute | solution.py:15
  71.3 7.1 %collective-permute-done.8 = f32[1,128,256]{2,1,0:T(8,128)S(1)} collective-permute-done((f32[1,128,256]{2,1,0:T(8,128)S(1)}, f32[1,128,256]{2,1,0:T(8,128)S(1)}, u32[]{:S(2)}, u32[]{:S(2)}) %collective-permute-start.8) | collective-permute-done | bytes 131104 | tf_op jit(solution)/shard_map/ppermute | solution.py:15
  78.4 7.1 %collective-permute-done.9 = f32[1,128,256]{2,1,0:T(8,128)S(1)} collective-permute-done((f32[1,128,256]{2,1,0:T(8,128)S(1)}, f32[1,128,256]{2,1,0:T(8,128)S(1)}, u32[]{:S(2)}, u32[]{:S(2)}) %collective-permute-start.9) | collective-permute-done | bytes 131104 | tf_op jit(solution)/shard_map/ppermute | solution.py:15
  113.9 8.5 %gather_fusion.2 = f32[6,24,128,128]{3,2,1,0:T(8,128)} fusion(f32[6,24,128,128]{3,2,1,0:T(8,128)} %param.17, s32[1024]{0:T(1024)S(1)} %pad_clamp_fusion.2), kind=kCustom, calls=%fused_computation.2 | custom fusion | bytes 18874392 | tf_op jit(solution)/shard_map/gather | solution.py:78
  133.1 9.7 %convolution_bitcast_fusion.3 = f32[2,128,256]{2,1,0:T(8,128)} fusion(f32[6,24,128,128]{3,2,1,0:T(8,128)} %gather_fusion.2, f32[2,24,128,256]{3,2,1,0:T(8,128)} %bitcast.81), kind=kOutput, calls=%fused_computation.33 | convolution fusion | flops 2415919104 | bytes 15990784 | tf_op jit(solution)/shard_map/rkab,rkbl->ral/dot_general | solution.py:26
  142.9 13.4 %reduce-scatter.5.cloned.1.call-done = f32[1,128,256]{2,1,0:T(8,128)} async-done(((f32[2,128,256]{2,1,0:T(8,128)}), f32[1,128,256]{2,1,0:T(8,128)}) %reduce-scatter.5.cloned.1.call-update) | async-done | bytes 131088 | tf_op jit(solution)/shard_map/reduce_scatter | solution.py:47
  164.6 7.1 %collective-permute-done.16 = f32[1,128,256]{2,1,0:T(8,128)S(1)} collective-permute-done((f32[1,128,256]{2,1,0:T(8,128)S(1)}, f32[1,128,256]{2,1,0:T(8,128)S(1)}, u32[]{:S(2)}, u32[]{:S(2)}) %collective-permute-start.16) | collective-permute-done | bytes 131104 | tf_op jit(solution)/shard_map/ppermute | solution.py:15
  171.7 7.1 %collective-permute-done.17 = f32[1,128,256]{2,1,0:T(8,128)S(1)} collective-permute-done((f32[1,128,256]{2,1,0:T(8,128)S(1)}, f32[1,128,256]{2,1,0:T(8,128)S(1)}, u32[]{:S(2)}, u32[]{:S(2)}) %collective-permute-start.17) | collective-permute-done | bytes 131104 | tf_op jit(solution)/shard_map/ppermute | solution.py:15
  178.8 7.1 %collective-permute-done.18 = f32[1,128,256]{2,1,0:T(8,128)S(1)} collective-permute-done((f32[1,128,256]{2,1,0:T(8,128)S(1)}, f32[1,128,256]{2,1,0:T(8,128)S(1)}, u32[]{:S(2)}, u32[]{:S(2)}) %collective-permute-start.18) | collective-permute-done | bytes 131104 | tf_op jit(solution)/shard_map/ppermute | solution.py:15
  185.9 7.1 %collective-permute-done.19 = f32[1,128,256]{2,1,0:T(8,128)S(1)} collective-permute-done((f32[1,128,256]{2,1,0:T(8,128)S(1)}, f32[1,128,256]{2,1,0:T(8,128)S(1)}, u32[]{:S(2)}, u32[]{:S(2)}) %collective-permute-start.19) | collective-permute-done | bytes 131104 | tf_op jit(solution)/shard_map/ppermute | solution.py:15
  193.0 7.1 %collective-permute-done.20 = f32[1,128,256]{2,1,0:T(8,128)S(1)} collective-permute-done((f32[1,128,256]{2,1,0:T(8,128)S(1)}, f32[1,128,256]{2,1,0:T(8,128)S(1)}, u32[]{:S(2)}, u32[]{:S(2)}) %collective-permute-start.20) | collective-permute-done | bytes 131104 | tf_op jit(solution)/shard_map/ppermute | solution.py:15
  200.1 7.1 %collective-permute-done.21 = f32[1,128,256]{2,1,0:T(8,128)S(1)} collective-permute-done((f32[1,128,256]{2,1,0:T(8,128)S(1)}, f32[1,128,256]{2,1,0:T(8,128)S(1)}, u32[]{:S(2)}, u32[]{:S(2)}) %collective-permute-start.21) | collective-permute-done | bytes 131104 | tf_op jit(solution)/shard_map/ppermute | solution.py:15
  207.2 7.1 %collective-permute-done.22 = f32[1,128,256]{2,1,0:T(8,128)S(1)} collective-permute-done((f32[1,128,256]{2,1,0:T(8,128)S(1)}, f32[1,128,256]{2,1,0:T(8,128)S(1)}, u32[]{:S(2)}, u32[]{:S(2)}) %collective-permute-start.22) | collective-permute-done | bytes 131104 | tf_op jit(solution)/shard_map/ppermute | solution.py:15
  214.3 7.1 %collective-permute-done.23 = f32[1,128,256]{2,1,0:T(8,128)S(1)} collective-permute-done((f32[1,128,256]{2,1,0:T(8,128)S(1)}, f32[1,128,256]{2,1,0:T(8,128)S(1)}, u32[]{:S(2)}, u32[]{:S(2)}) %collective-permute-start.23) | collective-permute-done | bytes 131104 | tf_op jit(solution)/shard_map/ppermute | solution.py:15
  221.4 7.1 %collective-permute-done.24 = f32[1,128,256]{2,1,0:T(8,128)S(1)} collective-permute-done((f32[1,128,256]{2,1,0:T(8,128)S(1)}, f32[1,128,256]{2,1,0:T(8,128)S(1)}, u32[]{:S(2)}, u32[]{:S(2)}) %collective-permute-start.24) | collective-permute-done | bytes 131104 | tf_op jit(solution)/shard_map/ppermute | solution.py:15
  228.4 7.1 %collective-permute-done.25 = f32[1,128,256]{2,1,0:T(8,128)S(1)} collective-permute-done((f32[1,128,256]{2,1,0:T(8,128)S(1)}, f32[1,128,256]{2,1,0:T(8,128)S(1)}, u32[]{:S(2)}, u32[]{:S(2)}) %collective-permute-start.25) | collective-permute-done | bytes 131104 | tf_op jit(solution)/shard_map/ppermute | solution.py:15
  235.5 7.1 %collective-permute-done.26 = f32[1,128,256]{2,1,0:T(8,128)S(1)} collective-permute-done((f32[1,128,256]{2,1,0:T(8,128)S(1)}, f32[1,128,256]{2,1,0:T(8,128)S(1)}, u32[]{:S(2)}, u32[]{:S(2)}) %collective-permute-start.26) | collective-permute-done | bytes 131104 | tf_op jit(solution)/shard_map/ppermute | solution.py:15
  242.6 7.1 %collective-permute-done.27 = f32[1,128,256]{2,1,0:T(8,128)S(1)} collective-permute-done((f32[1,128,256]{2,1,0:T(8,128)S(1)}, f32[1,128,256]{2,1,0:T(8,128)S(1)}, u32[]{:S(2)}, u32[]{:S(2)}) %collective-permute-start.27) | collective-permute-done | bytes 131104 | tf_op jit(solution)/shard_map/ppermute | solution.py:15
  272.6 9.7 %convolution_bitcast_fusion.2 = f32[2,128,256]{2,1,0:T(8,128)} fusion(f32[6,24,128,128]{3,2,1,0:T(8,128)} %gather_fusion.2, f32[2,24,128,256]{3,2,1,0:T(8,128)} %bitcast.79), kind=kOutput, calls=%fused_computation.32 | convolution fusion | flops 2415919104 | bytes 15990784 | tf_op jit(solution)/shard_map/rkab,rkbl->ral/dot_general | solution.py:26
  282.4 7.8 %reduce-scatter.7.cloned.1.call-done = f32[1,128,256]{2,1,0:T(8,128)} async-done(((f32[2,128,256]{2,1,0:T(8,128)}), f32[1,128,256]{2,1,0:T(8,128)}) %reduce-scatter.7.cloned.1.call-update) | async-done | bytes 131088 | tf_op jit(solution)/shard_map/reduce_scatter | solution.py:47
  298.5 7.1 %collective-permute-done.31 = f32[1,128,256]{2,1,0:T(8,128)S(1)} collective-permute-done((f32[1,128,256]{2,1,0:T(8,128)S(1)}, f32[1,128,256]{2,1,0:T(8,128)S(1)}, u32[]{:S(2)}, u32[]{:S(2)}) %collective-permute-start.31) | collective-permute-done | bytes 131104 | tf_op jit(solution)/shard_map/ppermute | solution.py:15
  305.6 7.1 %collective-permute-done.32 = f32[1,128,256]{2,1,0:T(8,128)S(1)} collective-permute-done((f32[1,128,256]{2,1,0:T(8,128)S(1)}, f32[1,128,256]{2,1,0:T(8,128)S(1)}, u32[]{:S(2)}, u32[]{:S(2)}) %collective-permute-start.32) | collective-permute-done | bytes 131104 | tf_op jit(solution)/shard_map/ppermute | solution.py:15
  312.7 7.1 %collective-permute-done.33 = f32[1,128,256]{2,1,0:T(8,128)S(1)} collective-permute-done((f32[1,128,256]{2,1,0:T(8,128)S(1)}, f32[1,128,256]{2,1,0:T(8,128)S(1)}, u32[]{:S(2)}, u32[]{:S(2)}) %collective-permute-start.33) | collective-permute-done | bytes 131104 | tf_op jit(solution)/shard_map/ppermute | solution.py:15
  319.8 7.1 %collective-permute-done.34 = f32[1,128,256]{2,1,0:T(8,128)S(1)} collective-permute-done((f32[1,128,256]{2,1,0:T(8,128)S(1)}, f32[1,128,256]{2,1,0:T(8,128)S(1)}, u32[]{:S(2)}, u32[]{:S(2)}) %collective-permute-start.34) | collective-permute-done | bytes 131104 | tf_op jit(solution)/shard_map/ppermute | solution.py:15
  326.9 7.1 %collective-permute-done.35 = f32[1,128,256]{2,1,0:T(8,128)S(1)} collective-permute-done((f32[1,128,256]{2,1,0:T(8,128)S(1)}, f32[1,128,256]{2,1,0:T(8,128)S(1)}, u32[]{:S(2)}, u32[]{:S(2)}) %collective-permute-start.35) | collective-permute-done | bytes 131104 | tf_op jit(solution)/shard_map/ppermute | solution.py:15
  334.0 7.1 %collective-permute-done.36 = f32[1,128,256]{2,1,0:T(8,128)S(1)} collective-permute-done((f32[1,128,256]{2,1,0:T(8,128)S(1)}, f32[1,128,256]{2,1,0:T(8,128)S(1)}, u32[]{:S(2)}, u32[]{:S(2)}) %collective-permute-start.36) | collective-permute-done | bytes 131104 | tf_op jit(solution)/shard_map/ppermute | solution.py:15
  341.1 7.1 %collective-permute-done.37 = f32[1,128,256]{2,1,0:T(8,128)S(1)} collective-permute-done((f32[1,128,256]{2,1,0:T(8,128)S(1)}, f32[1,128,256]{2,1,0:T(8,128)S(1)}, u32[]{:S(2)}, u32[]{:S(2)}) %collective-permute-start.37) | collective-permute-done | bytes 131104 | tf_op jit(solution)/shard_map/ppermute | solution.py:15
  348.2 7.1 %collective-permute-done.38 = f32[1,128,256]{2,1,0:T(8,128)S(1)} collective-permute-done((f32[1,128,256]{2,1,0:T(8,128)S(1)}, f32[1,128,256]{2,1,0:T(8,128)S(1)}, u32[]{:S(2)}, u32[]{:S(2)}) %collective-permute-start.38) | collective-permute-done | bytes 131104 | tf_op jit(solution)/shard_map/ppermute | solution.py:15
  355.2 7.1 %collective-permute-done.39 = f32[1,128,256]{2,1,0:T(8,128)S(1)} collective-permute-done((f32[1,128,256]{2,1,0:T(8,128)S(1)}, f32[1,128,256]{2,1,0:T(8,128)S(1)}, u32[]{:S(2)}, u32[]{:S(2)}) %collective-permute-start.39) | collective-permute-done | bytes 131104 | tf_op jit(solution)/shard_map/ppermute | solution.py:15
  362.3 7.1 %collective-permute-done.40 = f32[1,128,256]{2,1,0:T(8,128)S(1)} collective-permute-done((f32[1,128,256]{2,1,0:T(8,128)S(1)}, f32[1,128,256]{2,1,0:T(8,128)S(1)}, u32[]{:S(2)}, u32[]{:S(2)}) %collective-permute-start.40) | collective-permute-done | bytes 131104 | tf_op jit(solution)/shard_map/ppermute | solution.py:15
  369.4 7.1 %collective-permute-done.41 = f32[1,128,256]{2,1,0:T(8,128)S(1)} collective-permute-done((f32[1,128,256]{2,1,0:T(8,128)S(1)}, f32[1,128,256]{2,1,0:T(8,128)S(1)}, u32[]{:S(2)}, u32[]{:S(2)}) %collective-permute-start.41) | collective-permute-done | bytes 131104 | tf_op jit(solution)/shard_map/ppermute | solution.py:15
  376.5 7.1 %collective-permute-done.42 = f32[1,128,256]{2,1,0:T(8,128)S(1)} collective-permute-done((f32[1,128,256]{2,1,0:T(8,128)S(1)}, f32[1,128,256]{2,1,0:T(8,128)S(1)}, u32[]{:S(2)}, u32[]{:S(2)}) %collective-permute-start.42) | collective-permute-done | bytes 131104 | tf_op jit(solution)/shard_map/ppermute | solution.py:15
  383.6 7.1 %collective-permute-done.43 = f32[1,128,256]{2,1,0:T(8,128)S(1)} collective-permute-done((f32[1,128,256]{2,1,0:T(8,128)S(1)}, f32[1,128,256]{2,1,0:T(8,128)S(1)}, u32[]{:S(2)}, u32[]{:S(2)}) %collective-permute-start.43) | collective-permute-done | bytes 131104 | tf_op jit(solution)/shard_map/ppermute | solution.py:15
  390.7 7.1 %collective-permute-done.44 = f32[1,128,256]{2,1,0:T(8,128)S(1)} collective-permute-done((f32[1,128,256]{2,1,0:T(8,128)S(1)}, f32[1,128,256]{2,1,0:T(8,128)S(1)}, u32[]{:S(2)}, u32[]{:S(2)}) %collective-permute-start.44) | collective-permute-done | bytes 131104 | tf_op jit(solution)/shard_map/ppermute | solution.py:15
  406.4 9.7 %convolution_bitcast_fusion.1 = f32[2,128,256]{2,1,0:T(8,128)} fusion(f32[6,24,128,128]{3,2,1,0:T(8,128)} %gather_fusion.2, f32[2,24,128,256]{3,2,1,0:T(8,128)} %bitcast.80), kind=kOutput, calls=%fused_computation.31 | convolution fusion | flops 2415919104 | bytes 15990784 | tf_op jit(solution)/shard_map/rkab,rkbl->ral/dot_general | solution.py:26
  416.2 7.9 %reduce-scatter.9.cloned.1.call-done = f32[1,128,256]{2,1,0:T(8,128)} async-done(((f32[2,128,256]{2,1,0:T(8,128)}), f32[1,128,256]{2,1,0:T(8,128)}) %reduce-scatter.9.cloned.1.call-update) | async-done | bytes 131088 | tf_op jit(solution)/shard_map/reduce_scatter | solution.py:47
  432.4 7.1 %collective-permute-done.46 = f32[1,128,256]{2,1,0:T(8,128)S(1)} collective-permute-done((f32[1,128,256]{2,1,0:T(8,128)S(1)}, f32[1,128,256]{2,1,0:T(8,128)S(1)}, u32[]{:S(2)}, u32[]{:S(2)}) %collective-permute-start.46) | collective-permute-done | bytes 131104 | tf_op jit(solution)/shard_map/ppermute | solution.py:15
  439.5 7.1 %collective-permute-done.47 = f32[1,128,256]{2,1,0:T(8,128)S(1)} collective-permute-done((f32[1,128,256]{2,1,0:T(8,128)S(1)}, f32[1,128,256]{2,1,0:T(8,128)S(1)}, u32[]{:S(2)}, u32[]{:S(2)}) %collective-permute-start.47) | collective-permute-done | bytes 131104 | tf_op jit(solution)/shard_map/ppermute | solution.py:15
  446.5 7.1 %collective-permute-done.48 = f32[1,128,256]{2,1,0:T(8,128)S(1)} collective-permute-done((f32[1,128,256]{2,1,0:T(8,128)S(1)}, f32[1,128,256]{2,1,0:T(8,128)S(1)}, u32[]{:S(2)}, u32[]{:S(2)}) %collective-permute-start.48) | collective-permute-done | bytes 131104 | tf_op jit(solution)/shard_map/ppermute | solution.py:15
  460.7 7.1 %collective-permute-done.50 = f32[1,128,256]{2,1,0:T(8,128)S(1)} collective-permute-done((f32[1,128,256]{2,1,0:T(8,128)S(1)}, f32[1,128,256]{2,1,0:T(8,128)S(1)}, u32[]{:S(2)}, u32[]{:S(2)}) %collective-permute-start.50) | collective-permute-done | bytes 131104 | tf_op jit(solution)/shard_map/ppermute | solution.py:15
  540.3 9.8 %convolution_bitcast_fusion = f32[2,128,256]{2,1,0:T(8,128)} fusion(f32[6,24,128,128]{3,2,1,0:T(8,128)} %gather_fusion.2, f32[2,24,128,256]{3,2,1,0:T(8,128)} %bitcast.78), kind=kOutput, calls=%fused_computation.30 | convolution fusion | flops 2415919104 | bytes 15990784 | tf_op jit(solution)/shard_map/rkab,rkbl->ral/dot_general | solution.py:26
  (220 shorter events, 192.5 us)
Async XLA Ops:
  6.5 149.8 %reduce-scatter.5.cloned.1.call-start = ((), (), s32[]{:S(2)}) async-start(), calls=%async_computation.4 | async-start | bytes 393216 | tf_op jit(solution)/shard_map/reduce_scatter | solution.py:47
  13.5 8.1 %collective-permute-start = (f32[1,128,256]{2,1,0:T(8,128)S(1)}, f32[1,128,256]{2,1,0:T(8,128)S(1)}, u32[]{:S(2)}, u32[]{:S(2)}) collective-permute-start(f32[1,128,256]{2,1,0:T(8,128)S(1)} %convolution_bitcast_fusion.8), channel_id=1, source_target_pairs={{0,2},{2,4},{4,6},{6,8},{8,10},{10,12},{12,14},{14,16},{16,18},{18... | collective-permute-start | bytes 393224 | tf_op jit(solution)/shard_map/ppermute | solution.py:15
  21.6 7.1 %collective-permute-start.1 = (f32[1,128,256]{2,1,0:T(8,128)S(1)}, f32[1,128,256]{2,1,0:T(8,128)S(1)}, u32[]{:S(2)}, u32[]{:S(2)}) collective-permute-start(f32[1,128,256]{2,1,0:T(8,128)S(1)} %collective-permute-done), channel_id=1, source_target_pairs={{0,2},{2,4},{4,6},{6,8},{8,10},{10,12},{12,14},{14,16},{16,18},{18... | collective-permute-start | bytes 393224 | tf_op jit(solution)/shard_map/ppermute | solution.py:15
  28.7 7.1 %collective-permute-start.2 = (f32[1,128,256]{2,1,0:T(8,128)S(1)}, f32[1,128,256]{2,1,0:T(8,128)S(1)}, u32[]{:S(2)}, u32[]{:S(2)}) collective-permute-start(f32[1,128,256]{2,1,0:T(8,128)S(1)} %collective-permute-done.1), channel_id=1, source_target_pairs={{0,2},{2,4},{4,6},{6,8},{8,10},{10,12},{12,14},{14,16},{16,18},{18... | collective-permute-start | bytes 393224 | tf_op jit(solution)/shard_map/ppermute | solution.py:15
  35.8 7.1 %collective-permute-start.3 = (f32[1,128,256]{2,1,0:T(8,128)S(1)}, f32[1,128,256]{2,1,0:T(8,128)S(1)}, u32[]{:S(2)}, u32[]{:S(2)}) collective-permute-start(f32[1,128,256]{2,1,0:T(8,128)S(1)} %collective-permute-done.2), channel_id=1, source_target_pairs={{0,2},{2,4},{4,6},{6,8},{8,10},{10,12},{12,14},{14,16},{16,18},{18... | collective-permute-start | bytes 393224 | tf_op jit(solution)/shard_map/ppermute | solution.py:15
  42.9 7.1 %collective-permute-start.4 = (f32[1,128,256]{2,1,0:T(8,128)S(1)}, f32[1,128,256]{2,1,0:T(8,128)S(1)}, u32[]{:S(2)}, u32[]{:S(2)}) collective-permute-start(f32[1,128,256]{2,1,0:T(8,128)S(1)} %collective-permute-done.3), channel_id=1, source_target_pairs={{0,2},{2,4},{4,6},{6,8},{8,10},{10,12},{12,14},{14,16},{16,18},{18... | collective-permute-start | bytes 393224 | tf_op jit(solution)/shard_map/ppermute | solution.py:15
  50.0 7.1 %collective-permute-start.5 = (f32[1,128,256]{2,1,0:T(8,128)S(1)}, f32[1,128,256]{2,1,0:T(8,128)S(1)}, u32[]{:S(2)}, u32[]{:S(2)}) collective-permute-start(f32[1,128,256]{2,1,0:T(8,128)S(1)} %collective-permute-done.4), channel_id=1, source_target_pairs={{0,2},{2,4},{4,6},{6,8},{8,10},{10,12},{12,14},{14,16},{16,18},{18... | collective-permute-start | bytes 393224 | tf_op jit(solution)/shard_map/ppermute | solution.py:15
  57.1 7.1 %collective-permute-start.6 = (f32[1,128,256]{2,1,0:T(8,128)S(1)}, f32[1,128,256]{2,1,0:T(8,128)S(1)}, u32[]{:S(2)}, u32[]{:S(2)}) collective-permute-start(f32[1,128,256]{2,1,0:T(8,128)S(1)} %collective-permute-done.5), channel_id=1, source_target_pairs={{0,2},{2,4},{4,6},{6,8},{8,10},{10,12},{12,14},{14,16},{16,18},{18... | collective-permute-start | bytes 393224 | tf_op jit(solution)/shard_map/ppermute | solution.py:15
  64.2 7.1 %collective-permute-start.7 = (f32[1,128,256]{2,1,0:T(8,128)S(1)}, f32[1,128,256]{2,1,0:T(8,128)S(1)}, u32[]{:S(2)}, u32[]{:S(2)}) collective-permute-start(f32[1,128,256]{2,1,0:T(8,128)S(1)} %collective-permute-done.6), channel_id=1, source_target_pairs={{0,2},{2,4},{4,6},{6,8},{8,10},{10,12},{12,14},{14,16},{16,18},{18... | collective-permute-start | bytes 393224 | tf_op jit(solution)/shard_map/ppermute | solution.py:15
  71.3 7.1 %collective-permute-start.8 = (f32[1,128,256]{2,1,0:T(8,128)S(1)}, f32[1,128,256]{2,1,0:T(8,128)S(1)}, u32[]{:S(2)}, u32[]{:S(2)}) collective-permute-start(f32[1,128,256]{2,1,0:T(8,128)S(1)} %collective-permute-done.7), channel_id=1, source_target_pairs={{0,2},{2,4},{4,6},{6,8},{8,10},{10,12},{12,14},{14,16},{16,18},{18... | collective-permute-start | bytes 393224 | tf_op jit(solution)/shard_map/ppermute | solution.py:15
  78.4 7.1 %collective-permute-start.9 = (f32[1,128,256]{2,1,0:T(8,128)S(1)}, f32[1,128,256]{2,1,0:T(8,128)S(1)}, u32[]{:S(2)}, u32[]{:S(2)}) collective-permute-start(f32[1,128,256]{2,1,0:T(8,128)S(1)} %collective-permute-done.8), channel_id=1, source_target_pairs={{0,2},{2,4},{4,6},{6,8},{8,10},{10,12},{12,14},{14,16},{16,18},{18... | collective-permute-start | bytes 393224 | tf_op jit(solution)/shard_map/ppermute | solution.py:15
  85.5 7.1 %collective-permute-start.10 = (f32[1,128,256]{2,1,0:T(8,128)S(1)}, f32[1,128,256]{2,1,0:T(8,128)S(1)}, u32[]{:S(2)}, u32[]{:S(2)}) collective-permute-start(f32[1,128,256]{2,1,0:T(8,128)S(1)} %collective-permute-done.9), channel_id=1, source_target_pairs={{0,2},{2,4},{4,6},{6,8},{8,10},{10,12},{12,14},{14,16},{16,18},{18... | collective-permute-start | bytes 393224 | tf_op jit(solution)/shard_map/ppermute | solution.py:15
  92.6 7.1 %collective-permute-start.11 = (f32[1,128,256]{2,1,0:T(8,128)S(1)}, f32[1,128,256]{2,1,0:T(8,128)S(1)}, u32[]{:S(2)}, u32[]{:S(2)}) collective-permute-start(f32[1,128,256]{2,1,0:T(8,128)S(1)} %collective-permute-done.10), channel_id=1, source_target_pairs={{0,2},{2,4},{4,6},{6,8},{8,10},{10,12},{12,14},{14,16},{16,18},{18... | collective-permute-start | bytes 393224 | tf_op jit(solution)/shard_map/ppermute | solution.py:15
  99.6 7.1 %collective-permute-start.12 = (f32[1,128,256]{2,1,0:T(8,128)S(1)}, f32[1,128,256]{2,1,0:T(8,128)S(1)}, u32[]{:S(2)}, u32[]{:S(2)}) collective-permute-start(f32[1,128,256]{2,1,0:T(8,128)S(1)} %collective-permute-done.11), channel_id=1, source_target_pairs={{0,2},{2,4},{4,6},{6,8},{8,10},{10,12},{12,14},{14,16},{16,18},{18... | collective-permute-start | bytes 393224 | tf_op jit(solution)/shard_map/ppermute | solution.py:15
  106.7 7.1 %collective-permute-start.13 = (f32[1,128,256]{2,1,0:T(8,128)S(1)}, f32[1,128,256]{2,1,0:T(8,128)S(1)}, u32[]{:S(2)}, u32[]{:S(2)}) collective-permute-start(f32[1,128,256]{2,1,0:T(8,128)S(1)} %collective-permute-done.12), channel_id=1, source_target_pairs={{0,2},{2,4},{4,6},{6,8},{8,10},{10,12},{12,14},{14,16},{16,18},{18... | collective-permute-start | bytes 393224 | tf_op jit(solution)/shard_map/ppermute | solution.py:15
  113.8 8.6 %collective-permute-start.14 = (f32[1,128,256]{2,1,0:T(8,128)S(1)}, f32[1,128,256]{2,1,0:T(8,128)S(1)}, u32[]{:S(2)}, u32[]{:S(2)}) collective-permute-start(f32[1,128,256]{2,1,0:T(8,128)S(1)} %collective-permute-done.13), channel_id=1, source_target_pairs={{0,2},{2,4},{4,6},{6,8},{8,10},{10,12},{12,14},{14,16},{16,18},{18... | collective-permute-start | bytes 393224 | tf_op jit(solution)/shard_map/ppermute | solution.py:15
  142.9 147.3 %reduce-scatter.7.cloned.1.call-start = ((), (), s32[]{:S(2)}) async-start(), calls=%async_computation.5 | async-start | bytes 393216 | tf_op jit(solution)/shard_map/reduce_scatter | solution.py:47
  157.5 7.1 %collective-permute-start.15 = (f32[1,128,256]{2,1,0:T(8,128)S(1)}, f32[1,128,256]{2,1,0:T(8,128)S(1)}, u32[]{:S(2)}, u32[]{:S(2)}) collective-permute-start(f32[1,128,256]{2,1,0:T(8,128)S(1)} %convolution_bitcast_fusion.7), channel_id=1, source_target_pairs={{0,2},{2,4},{4,6},{6,8},{8,10},{10,12},{12,14},{14,16},{16,18},{18... | collective-permute-start | bytes 393224 | tf_op jit(solution)/shard_map/ppermute | solution.py:15
  164.6 7.1 %collective-permute-start.16 = (f32[1,128,256]{2,1,0:T(8,128)S(1)}, f32[1,128,256]{2,1,0:T(8,128)S(1)}, u32[]{:S(2)}, u32[]{:S(2)}) collective-permute-start(f32[1,128,256]{2,1,0:T(8,128)S(1)} %collective-permute-done.15), channel_id=1, source_target_pairs={{0,2},{2,4},{4,6},{6,8},{8,10},{10,12},{12,14},{14,16},{16,18},{18... | collective-permute-start | bytes 393224 | tf_op jit(solution)/shard_map/ppermute | solution.py:15
  171.7 7.1 %collective-permute-start.17 = (f32[1,128,256]{2,1,0:T(8,128)S(1)}, f32[1,128,256]{2,1,0:T(8,128)S(1)}, u32[]{:S(2)}, u32[]{:S(2)}) collective-permute-start(f32[1,128,256]{2,1,0:T(8,128)S(1)} %collective-permute-done.16), channel_id=1, source_target_pairs={{0,2},{2,4},{4,6},{6,8},{8,10},{10,12},{12,14},{14,16},{16,18},{18... | collective-permute-start | bytes 393224 | tf_op jit(solution)/shard_map/ppermute | solution.py:15
  178.8 7.1 %collective-permute-start.18 = (f32[1,128,256]{2,1,0:T(8,128)S(1)}, f32[1,128,256]{2,1,0:T(8,128)S(1)}, u32[]{:S(2)}, u32[]{:S(2)}) collective-permute-start(f32[1,128,256]{2,1,0:T(8,128)S(1)} %collective-permute-done.17), channel_id=1, source_target_pairs={{0,2},{2,4},{4,6},{6,8},{8,10},{10,12},{12,14},{14,16},{16,18},{18... | collective-permute-start | bytes 393224 | tf_op jit(solution)/shard_map/ppermute | solution.py:15
  185.9 7.1 %collective-permute-start.19 = (f32[1,128,256]{2,1,0:T(8,128)S(1)}, f32[1,128,256]{2,1,0:T(8,128)S(1)}, u32[]{:S(2)}, u32[]{:S(2)}) collective-permute-start(f32[1,128,256]{2,1,0:T(8,128)S(1)} %collective-permute-done.18), channel_id=1, source_target_pairs={{0,2},{2,4},{4,6},{6,8},{8,10},{10,12},{12,14},{14,16},{16,18},{18... | collective-permute-start | bytes 393224 | tf_op jit(solution)/shard_map/ppermute | solution.py:15
  193.0 7.1 %collective-permute-start.20 = (f32[1,128,256]{2,1,0:T(8,128)S(1)}, f32[1,128,256]{2,1,0:T(8,128)S(1)}, u32[]{:S(2)}, u32[]{:S(2)}) collective-permute-start(f32[1,128,256]{2,1,0:T(8,128)S(1)} %collective-permute-done.19), channel_id=1, source_target_pairs={{0,2},{2,4},{4,6},{6,8},{8,10},{10,12},{12,14},{14,16},{16,18},{18... | collective-permute-start | bytes 393224 | tf_op jit(solution)/shard_map/ppermute | solution.py:15
  200.1 7.1 %collective-permute-start.21 = (f32[1,128,256]{2,1,0:T(8,128)S(1)}, f32[1,128,256]{2,1,0:T(8,128)S(1)}, u32[]{:S(2)}, u32[]{:S(2)}) collective-permute-start(f32[1,128,256]{2,1,0:T(8,128)S(1)} %collective-permute-done.20), channel_id=1, source_target_pairs={{0,2},{2,4},{4,6},{6,8},{8,10},{10,12},{12,14},{14,16},{16,18},{18... | collective-permute-start | bytes 393224 | tf_op jit(solution)/shard_map/ppermute | solution.py:15
  207.2 7.1 %collective-permute-start.22 = (f32[1,128,256]{2,1,0:T(8,128)S(1)}, f32[1,128,256]{2,1,0:T(8,128)S(1)}, u32[]{:S(2)}, u32[]{:S(2)}) collective-permute-start(f32[1,128,256]{2,1,0:T(8,128)S(1)} %collective-permute-done.21), channel_id=1, source_target_pairs={{0,2},{2,4},{4,6},{6,8},{8,10},{10,12},{12,14},{14,16},{16,18},{18... | collective-permute-start | bytes 393224 | tf_op jit(solution)/shard_map/ppermute | solution.py:15
  214.3 7.1 %collective-permute-start.23 = (f32[1,128,256]{2,1,0:T(8,128)S(1)}, f32[1,128,256]{2,1,0:T(8,128)S(1)}, u32[]{:S(2)}, u32[]{:S(2)}) collective-permute-start(f32[1,128,256]{2,1,0:T(8,128)S(1)} %collective-permute-done.22), channel_id=1, source_target_pairs={{0,2},{2,4},{4,6},{6,8},{8,10},{10,12},{12,14},{14,16},{16,18},{18... | collective-permute-start | bytes 393224 | tf_op jit(solution)/shard_map/ppermute | solution.py:15
  221.3 7.1 %collective-permute-start.24 = (f32[1,128,256]{2,1,0:T(8,128)S(1)}, f32[1,128,256]{2,1,0:T(8,128)S(1)}, u32[]{:S(2)}, u32[]{:S(2)}) collective-permute-start(f32[1,128,256]{2,1,0:T(8,128)S(1)} %collective-permute-done.23), channel_id=1, source_target_pairs={{0,2},{2,4},{4,6},{6,8},{8,10},{10,12},{12,14},{14,16},{16,18},{18... | collective-permute-start | bytes 393224 | tf_op jit(solution)/shard_map/ppermute | solution.py:15
  228.4 7.1 %collective-permute-start.25 = (f32[1,128,256]{2,1,0:T(8,128)S(1)}, f32[1,128,256]{2,1,0:T(8,128)S(1)}, u32[]{:S(2)}, u32[]{:S(2)}) collective-permute-start(f32[1,128,256]{2,1,0:T(8,128)S(1)} %collective-permute-done.24), channel_id=1, source_target_pairs={{0,2},{2,4},{4,6},{6,8},{8,10},{10,12},{12,14},{14,16},{16,18},{18... | collective-permute-start | bytes 393224 | tf_op jit(solution)/shard_map/ppermute | solution.py:15
  235.5 7.1 %collective-permute-start.26 = (f32[1,128,256]{2,1,0:T(8,128)S(1)}, f32[1,128,256]{2,1,0:T(8,128)S(1)}, u32[]{:S(2)}, u32[]{:S(2)}) collective-permute-start(f32[1,128,256]{2,1,0:T(8,128)S(1)} %collective-permute-done.25), channel_id=1, source_target_pairs={{0,2},{2,4},{4,6},{6,8},{8,10},{10,12},{12,14},{14,16},{16,18},{18... | collective-permute-start | bytes 393224 | tf_op jit(solution)/shard_map/ppermute | solution.py:15
  242.6 7.1 %collective-permute-start.27 = (f32[1,128,256]{2,1,0:T(8,128)S(1)}, f32[1,128,256]{2,1,0:T(8,128)S(1)}, u32[]{:S(2)}, u32[]{:S(2)}) collective-permute-start(f32[1,128,256]{2,1,0:T(8,128)S(1)} %collective-permute-done.26), channel_id=1, source_target_pairs={{0,2},{2,4},{4,6},{6,8},{8,10},{10,12},{12,14},{14,16},{16,18},{18... | collective-permute-start | bytes 393224 | tf_op jit(solution)/shard_map/ppermute | solution.py:15
  249.7 7.1 %collective-permute-start.28 = (f32[1,128,256]{2,1,0:T(8,128)S(1)}, f32[1,128,256]{2,1,0:T(8,128)S(1)}, u32[]{:S(2)}, u32[]{:S(2)}) collective-permute-start(f32[1,128,256]{2,1,0:T(8,128)S(1)} %collective-permute-done.27), channel_id=1, source_target_pairs={{0,2},{2,4},{4,6},{6,8},{8,10},{10,12},{12,14},{14,16},{16,18},{18... | collective-permute-start | bytes 393224 | tf_op jit(solution)/shard_map/ppermute | solution.py:15
  256.8 7.1 %collective-permute-start.29 = (f32[1,128,256]{2,1,0:T(8,128)S(1)}, f32[1,128,256]{2,1,0:T(8,128)S(1)}, u32[]{:S(2)}, u32[]{:S(2)}) collective-permute-start(f32[1,128,256]{2,1,0:T(8,128)S(1)} %collective-permute-done.28), channel_id=1, source_target_pairs={{0,2},{2,4},{4,6},{6,8},{8,10},{10,12},{12,14},{14,16},{16,18},{18... | collective-permute-start | bytes 393224 | tf_op jit(solution)/shard_map/ppermute | solution.py:15
  282.3 141.7 %reduce-scatter.9.cloned.1.call-start = ((), (), s32[]{:S(2)}) async-start(), calls=%async_computation.6 | async-start | bytes 393216 | tf_op jit(solution)/shard_map/reduce_scatter | solution.py:47
  291.4 7.1 %collective-permute-start.30 = (f32[1,128,256]{2,1,0:T(8,128)S(1)}, f32[1,128,256]{2,1,0:T(8,128)S(1)}, u32[]{:S(2)}, u32[]{:S(2)}) collective-permute-start(f32[1,128,256]{2,1,0:T(8,128)S(1)} %convolution_bitcast_fusion.6), channel_id=1, source_target_pairs={{0,2},{2,4},{4,6},{6,8},{8,10},{10,12},{12,14},{14,16},{16,18},{18... | collective-permute-start | bytes 393224 | tf_op jit(solution)/shard_map/ppermute | solution.py:15
  298.5 7.1 %collective-permute-start.31 = (f32[1,128,256]{2,1,0:T(8,128)S(1)}, f32[1,128,256]{2,1,0:T(8,128)S(1)}, u32[]{:S(2)}, u32[]{:S(2)}) collective-permute-start(f32[1,128,256]{2,1,0:T(8,128)S(1)} %collective-permute-done.30), channel_id=1, source_target_pairs={{0,2},{2,4},{4,6},{6,8},{8,10},{10,12},{12,14},{14,16},{16,18},{18... | collective-permute-start | bytes 393224 | tf_op jit(solution)/shard_map/ppermute | solution.py:15
  305.6 7.1 %collective-permute-start.32 = (f32[1,128,256]{2,1,0:T(8,128)S(1)}, f32[1,128,256]{2,1,0:T(8,128)S(1)}, u32[]{:S(2)}, u32[]{:S(2)}) collective-permute-start(f32[1,128,256]{2,1,0:T(8,128)S(1)} %collective-permute-done.31), channel_id=1, source_target_pairs={{0,2},{2,4},{4,6},{6,8},{8,10},{10,12},{12,14},{14,16},{16,18},{18... | collective-permute-start | bytes 393224 | tf_op jit(solution)/shard_map/ppermute | solution.py:15
  312.7 7.1 %collective-permute-start.33 = (f32[1,128,256]{2,1,0:T(8,128)S(1)}, f32[1,128,256]{2,1,0:T(8,128)S(1)}, u32[]{:S(2)}, u32[]{:S(2)}) collective-permute-start(f32[1,128,256]{2,1,0:T(8,128)S(1)} %collective-permute-done.32), channel_id=1, source_target_pairs={{0,2},{2,4},{4,6},{6,8},{8,10},{10,12},{12,14},{14,16},{16,18},{18... | collective-permute-start | bytes 393224 | tf_op jit(solution)/shard_map/ppermute | solution.py:15
  319.8 7.1 %collective-permute-start.34 = (f32[1,128,256]{2,1,0:T(8,128)S(1)}, f32[1,128,256]{2,1,0:T(8,128)S(1)}, u32[]{:S(2)}, u32[]{:S(2)}) collective-permute-start(f32[1,128,256]{2,1,0:T(8,128)S(1)} %collective-permute-done.33), channel_id=1, source_target_pairs={{0,2},{2,4},{4,6},{6,8},{8,10},{10,12},{12,14},{14,16},{16,18},{18... | collective-permute-start | bytes 393224 | tf_op jit(solution)/shard_map/ppermute | solution.py:15
  326.9 7.1 %collective-permute-start.35 = (f32[1,128,256]{2,1,0:T(8,128)S(1)}, f32[1,128,256]{2,1,0:T(8,128)S(1)}, u32[]{:S(2)}, u32[]{:S(2)}) collective-permute-start(f32[1,128,256]{2,1,0:T(8,128)S(1)} %collective-permute-done.34), channel_id=1, source_target_pairs={{0,2},{2,4},{4,6},{6,8},{8,10},{10,12},{12,14},{14,16},{16,18},{18... | collective-permute-start | bytes 393224 | tf_op jit(solution)/shard_map/ppermute | solution.py:15
  334.0 7.1 %collective-permute-start.36 = (f32[1,128,256]{2,1,0:T(8,128)S(1)}, f32[1,128,256]{2,1,0:T(8,128)S(1)}, u32[]{:S(2)}, u32[]{:S(2)}) collective-permute-start(f32[1,128,256]{2,1,0:T(8,128)S(1)} %collective-permute-done.35), channel_id=1, source_target_pairs={{0,2},{2,4},{4,6},{6,8},{8,10},{10,12},{12,14},{14,16},{16,18},{18... | collective-permute-start | bytes 393224 | tf_op jit(solution)/shard_map/ppermute | solution.py:15
  341.1 7.1 %collective-permute-start.37 = (f32[1,128,256]{2,1,0:T(8,128)S(1)}, f32[1,128,256]{2,1,0:T(8,128)S(1)}, u32[]{:S(2)}, u32[]{:S(2)}) collective-permute-start(f32[1,128,256]{2,1,0:T(8,128)S(1)} %collective-permute-done.36), channel_id=1, source_target_pairs={{0,2},{2,4},{4,6},{6,8},{8,10},{10,12},{12,14},{14,16},{16,18},{18... | collective-permute-start | bytes 393224 | tf_op jit(solution)/shard_map/ppermute | solution.py:15
  348.2 7.1 %collective-permute-start.38 = (f32[1,128,256]{2,1,0:T(8,128)S(1)}, f32[1,128,256]{2,1,0:T(8,128)S(1)}, u32[]{:S(2)}, u32[]{:S(2)}) collective-permute-start(f32[1,128,256]{2,1,0:T(8,128)S(1)} %collective-permute-done.37), channel_id=1, source_target_pairs={{0,2},{2,4},{4,6},{6,8},{8,10},{10,12},{12,14},{14,16},{16,18},{18... | collective-permute-start | bytes 393224 | tf_op jit(solution)/shard_map/ppermute | solution.py:15
  355.2 7.1 %collective-permute-start.39 = (f32[1,128,256]{2,1,0:T(8,128)S(1)}, f32[1,128,256]{2,1,0:T(8,128)S(1)}, u32[]{:S(2)}, u32[]{:S(2)}) collective-permute-start(f32[1,128,256]{2,1,0:T(8,128)S(1)} %collective-permute-done.38), channel_id=1, source_target_pairs={{0,2},{2,4},{4,6},{6,8},{8,10},{10,12},{12,14},{14,16},{16,18},{18... | collective-permute-start | bytes 393224 | tf_op jit(solution)/shard_map/ppermute | solution.py:15
  362.3 7.1 %collective-permute-start.40 = (f32[1,128,256]{2,1,0:T(8,128)S(1)}, f32[1,128,256]{2,1,0:T(8,128)S(1)}, u32[]{:S(2)}, u32[]{:S(2)}) collective-permute-start(f32[1,128,256]{2,1,0:T(8,128)S(1)} %collective-permute-done.39), channel_id=1, source_target_pairs={{0,2},{2,4},{4,6},{6,8},{8,10},{10,12},{12,14},{14,16},{16,18},{18... | collective-permute-start | bytes 393224 | tf_op jit(solution)/shard_map/ppermute | solution.py:15
  369.4 7.1 %collective-permute-start.41 = (f32[1,128,256]{2,1,0:T(8,128)S(1)}, f32[1,128,256]{2,1,0:T(8,128)S(1)}, u32[]{:S(2)}, u32[]{:S(2)}) collective-permute-start(f32[1,128,256]{2,1,0:T(8,128)S(1)} %collective-permute-done.40), channel_id=1, source_target_pairs={{0,2},{2,4},{4,6},{6,8},{8,10},{10,12},{12,14},{14,16},{16,18},{18... | collective-permute-start | bytes 393224 | tf_op jit(solution)/shard_map/ppermute | solution.py:15
  416.1 141.9 %reduce-scatter.11.cloned.1.call-start = ((), (), s32[]{:S(2)}) async-start(), calls=%async_computation.7 | async-start | bytes 393216 | tf_op jit(solution)/shard_map/reduce_scatter | solution.py:47
  425.2 7.1 %collective-permute-start.45 = (f32[1,128,256]{2,1,0:T(8,128)S(1)}, f32[1,128,256]{2,1,0:T(8,128)S(1)}, u32[]{:S(2)}, u32[]{:S(2)}) collective-permute-start(f32[1,128,256]{2,1,0:T(8,128)S(1)} %convolution_bitcast_fusion.5), channel_id=1, source_target_pairs={{0,2},{2,4},{4,6},{6,8},{8,10},{10,12},{12,14},{14,16},{16,18},{18... | collective-permute-start | bytes 393224 | tf_op jit(solution)/shard_map/ppermute | solution.py:15
  489.1 7.1 %collective-permute-start.54 = (f32[1,128,256]{2,1,0:T(8,128)S(1)}, f32[1,128,256]{2,1,0:T(8,128)S(1)}, u32[]{:S(2)}, u32[]{:S(2)}) collective-permute-start(f32[1,128,256]{2,1,0:T(8,128)S(1)} %collective-permute-done.53), channel_id=1, source_target_pairs={{0,2},{2,4},{4,6},{6,8},{8,10},{10,12},{12,14},{14,16},{16,18},{18... | collective-permute-start | bytes 393224 | tf_op jit(solution)/shard_map/ppermute | solution.py:15
  (19 other events, 219.5 us)
Sparse Core Ops, SparseCore 0:
  143.0 13.2 reduce-scatter.4
  282.4 7.7 reduce-scatter.6
  416.2 7.7 reduce-scatter.8
  550.2 7.7 reduce-scatter.10
